TPU v7x, 32 devices: a whole 2x2x4 slice. The times are simulated.
32 devices in a mesh: sub: 8 (over z, x), grp: 4 (over y, core).
Axes of the slice: x: 2, y: 2, z: 4, core: 2. Of those that a mesh axis runs over, the one named last changes fastest.
Arguments:
- loads: float32 [4, 16, 2, 48, 256], P('grp', 'sub'), may hold values from -18 to 18
- inv_schur: bfloat16 [4, 16, 1024, 1024], P('grp', 'sub'), as said below
- schur: bfloat16 [4, 16, 1024, 1024], P('grp', 'sub'), as said below
- coarse_map: bfloat16 [4, 16, 12, 1024], P('grp', 'sub'), may hold values from -0.75 to 0.75
- coarse_inverse: float32 [4, 16, 12, 4, 192], P('grp', 'sub'), as said below
- face_rows: int32 [4, 16, 1024], P('grp', 'sub'), may hold values from 0 to 1023, each once within a row
- face_len: int32 [4, 16, 2], P('grp', 'sub'), may hold values from 64 to 256
Outputs:
- multipliers: float32 [4, 16, 2, 48, 256], P('grp', 'sub')
- residual: float32 [4, 16, 2, 48, 256], P('grp', 'sub')
Inputs may be any that keep to these rules, and one draw needn't show every extreme that they name: `inv_schur`: each subdomain's matrix is symmetric and positive definite. `schur`: each subdomain's matrix is symmetric and positive definite. `coarse_inverse`: seen as a [768, 768] matrix it is symmetric and positive definite. `face_rows`: each subdomain's row is a permutation of 0 to 1023.
All inputs are finite; a program needn't handle non-finite values.
Results may differ from a plain program's by a relative error of at most 0.025.
Values sent between devices are 32-bit elements; how exact they have to be, the bound alone decides.
A program may use at most 128 MiB of HBM per device.

v0:
```python
import jax
import jax.numpy as jnp
from jax import lax
from jax.sharding import PartitionSpec as P

FACE = 256
LOADS = 48
CDOF = 12
ITERS = 3


def shifted(value, axis, steps):
    count = lax.axis_size(axis)
    initial, last = (max(0, -steps), min(count, count - steps))
    return lax.ppermute(value, axis, [(source, source + steps) for source in range(initial, last)])


def passed_along(block, axis, distance):
    devices = range(lax.axis_size(axis))
    route = [((i - distance) % len(devices), i) for i in devices]
    return lax.ppermute(block, axis, route)


def pair_sum(first, second, pattern):
    return jnp.einsum(pattern, first, second, precision=lax.Precision.HIGHEST)


def combine(weights, faces):
    return jnp.einsum("ab,gksat->gksbt", weights, faces, precision=lax.Precision.HIGHEST)


def gram_solve(matrix, right):
    return jax.scipy.linalg.cho_solve((jnp.linalg.cholesky(matrix), True), right)


def to_slots(faces):
    along = faces[0, :, 0]
    beside_all = faces[0, :, 1]
    from_left = shifted(along[1:2], "sub", 1)
    from_left = jnp.concatenate([from_left, along[0:1]], axis=0)
    from_below = passed_along(beside_all, "grp", 1)
    stacked = jnp.stack([-from_left, along, -from_below, beside_all], axis=2)
    return stacked.reshape(stacked.shape[0], stacked.shape[1], -1)


def to_faces(field, live_mask):
    pieces = field.reshape(field.shape[0], field.shape[1], 4, -1)
    from_right = shifted(pieces[0:1, :, 0], "sub", -1)
    neighbour = jnp.concatenate([pieces[1:2, :, 0], from_right], axis=0)
    from_above = passed_along(pieces[:, :, 2], "grp", -1)
    jumps = jnp.stack([pieces[:, :, 1] - neighbour, pieces[:, :, 3] - from_above], axis=1)
    return jumps[None] * live_mask


def body(loads, inv_schur, schur, coarse_map, coarse_inverse, face_rows, face_len):
    slot_rows = face_rows[0]
    permute = jax.vmap(lambda matrix, ordering: matrix[ordering][:, ordering])
    solve_mats = permute(inv_schur[0], slot_rows)
    dirichlet = permute(schur[0], slot_rows)
    coarse_basis = jax.vmap(lambda basis_rows, ordering: basis_rows[:, ordering])(
        coarse_map[0], slot_rows
    )
    own_rows = coarse_inverse[0].reshape(2 * CDOF, coarse_inverse.shape[3], coarse_inverse.shape[4])
    positions = jnp.arange(FACE)
    column = 2 * lax.axis_index("sub") + jnp.arange(2)
    last_column = 2 * lax.axis_size("sub") - 1
    along_live = (positions[None, :] < face_len[0, :, 0:1]) & (column[:, None] < last_column)
    around_live = positions[None, :] < face_len[0, :, 1:2]
    live_mask = jnp.stack([along_live, around_live], axis=1).astype(jnp.float32)[
        None, :, :, None, :
    ]

    def precondition(resid):
        slotted = to_slots(resid)
        smoothed = jnp.einsum(
            "krm,kmn->krn",
            slotted.astype(jnp.bfloat16),
            dirichlet,
            preferred_element_type=jnp.float32,
        )
        filtered = to_faces(smoothed, live_mask)
        product = lax.psum(pair_sum(filtered, resid, "gksat,gksbt->ab"), ("sub", "grp"))
        return (filtered, product)

    residual = loads * live_mask
    multipliers = jnp.zeros_like(residual)
    search, precond_gram = precondition(residual)
    direction = search
    for iteration in range(ITERS):
        operator_slotted = to_slots(direction)
        rounded = operator_slotted.astype(jnp.bfloat16)
        local_part = jnp.einsum(
            "krm,kmn->krn", rounded, solve_mats, preferred_element_type=jnp.float32
        )
        operator_coarse_terms = jnp.einsum(
            "krm,kqm->krq", rounded, coarse_basis, preferred_element_type=jnp.float32
        )
        flat_terms = jnp.transpose(operator_coarse_terms, (1, 0, 2)).reshape(1, LOADS, 2 * CDOF)
        cycle_terms = lax.all_gather(flat_terms, "grp", axis=0, tiled=True)
        solved = jnp.einsum(
            "grx,kgx->rk",
            lax.all_gather(cycle_terms, "sub", axis=2, tiled=True),
            own_rows,
            precision=lax.Precision.HIGHEST,
        )
        corrections = jnp.transpose(solved.reshape(LOADS, 2, CDOF), (1, 0, 2)).astype(jnp.bfloat16)
        response = local_part + jnp.einsum(
            "krq,kqm->krm", corrections, coarse_basis, preferred_element_type=jnp.float32
        )
        image_faces = to_faces(response, live_mask)
        curvature = lax.psum(pair_sum(direction, image_faces, "gksat,gksbt->ab"), ("sub", "grp"))
        image_faces, curvature = (image_faces, curvature)
        step_size = gram_solve(curvature, precond_gram)
        multipliers = multipliers + combine(step_size, direction)
        residual = residual - combine(step_size, image_faces)
        if iteration + 1 < ITERS:
            search, new_gram = precondition(residual)
            conjugate = gram_solve(precond_gram, new_gram)
            direction = search + combine(conjugate, direction)
            precond_gram = new_gram
    return (multipliers, residual)


def solution(mesh):
    in_specs = (
        P("grp", "sub", None, None, None),
        P("grp", "sub", None, None),
        P("grp", "sub", None, None),
        P("grp", "sub", None, None),
        P("grp", "sub", None, None, None),
        P("grp", "sub", None),
        P("grp", "sub", None),
    )
    out_specs = (P("grp", "sub", None, None, None), P("grp", "sub", None, None, None))
    return jax.shard_map(body, mesh=mesh, in_specs=in_specs, out_specs=out_specs, check_vma=False)
```

profile of v0, /device:TPU:10, one launch (start us, length us, event | category | flops | bytes accessed | tf_op | source)
XLA Modules:
  0.0 658.3 jit_solution(1124318638356162383)
XLA Ops:
  7.0 41.9 %gather_fusion = bf16[2048,1024]{1,0:T(8,128)(2,1)} fusion(bf16[2,1024,1024]{2,1,0:T(8,128)(2,1)} %bitcast.533, s32[2048]{0:T(1024)S(1)} %bitcast.528), kind=kCustom, calls=%fused_computation | custom fusion | bytes 8404992 | tf_op jit(solution)/shard_map/vmap()/gather | solution.py:57
  48.9 6.2 copy.171
  55.2 40.3 %gather_fusion.1 = bf16[2048,1024]{1,0:T(8,128)(2,1)} fusion(bf16[2,1024,1024]{1,2,0:T(8,128)(2,1)} %copy.171, s32[2048]{0:T(1024)S(1)} %bitcast.529), kind=kCustom, calls=%fused_computation.1 | custom fusion | bytes 8404992 | tf_op jit(solution)/shard_map/vmap()/gather | solution.py:57
  95.5 42.0 %gather_fusion.2 = bf16[2048,1024]{1,0:T(8,128)(2,1)} fusion(bf16[2,1024,1024]{2,1,0:T(8,128)(2,1)} %bitcast.534, s32[2048]{0:T(1024)S(1)} %bitcast.530), kind=kCustom, calls=%fused_computation.2 | custom fusion | bytes 8404992 | tf_op jit(solution)/shard_map/vmap()/gather | solution.py:57
  137.5 6.2 copy.182
  143.8 40.4 %gather_fusion.3 = bf16[2048,1024]{1,0:T(8,128)(2,1)} fusion(bf16[2,1024,1024]{1,2,0:T(8,128)(2,1)} %copy.182, s32[2048]{0:T(1024)S(1)} %bitcast.531), kind=kCustom, calls=%fused_computation.3 | custom fusion | bytes 8404992 | tf_op jit(solution)/shard_map/vmap()/gather | solution.py:57
  184.5 11.1 %gather_fusion.4 = bf16[2048,12]{1,0:T(8,128)(2,1)S(1)} fusion(bf16[2,12,1024]{1,2,0:T(8,128)(2,1)S(1)} %bitcast.549, s32[2048]{0:T(1024)S(1)} %bitcast.532), kind=kCustom, calls=%fused_computation.4 | custom fusion | bytes 114688 | tf_op jit(solution)/shard_map/vmap()/gather | solution.py:60
  216.7 5.2 all_gather.18
  221.9 26.2 %all_gather.19 = f32[4,48,192]{1,2,0:T(8,128)S(1)} all-gather(f32[4,48,24]{1,2,0:T(8,128)S(1)} %all_gather.18), channel_id=1, replica_groups=mesh['sub'=8,'grp'=4] {'sub'}, dimensions={2}, use_global_device_ids=true | all-gather | bytes 165888 | tf_op jit(solution)/shard_map/all_gather | solution.py:102
  256.8 43.6 %all-reduce = (f32[48,48]{0,1:T(8,128)S(1)}, f32[48,48]{0,1:T(8,128)S(1)}) all-reduce(f32[48,48]{0,1:T(8,128)S(1)} %convolution_bitcast_fusion.14, f32[48,48]{0,1:T(8,128)S(1)} %convolution_bitcast_fusion.15), channel_id=1, replica_groups=mesh['sub'=8,'grp'=4] {'sub','grp'}, use_global_device_ids=true, to_apply=%region_3.5 | all-reduce | flops 4608 | bytes 36864 | tf_op jit(solution)/shard_map/psum | solution.py:82
  300.6 4.4 cholesky.89
  313.2 4.4 cholesky.100
  334.8 40.7 %psum.44 = f32[48,48]{0,1:T(8,128)S(1)} all-reduce(f32[48,48]{0,1:T(8,128)S(1)} %convolution_bitcast_fusion.13), channel_id=1, replica_groups=mesh['sub'=8,'grp'=4] {'sub','grp'}, use_global_device_ids=true, to_apply=%region_4.0 | all-reduce | flops 2304 | bytes 18432 | tf_op jit(solution)/shard_map/psum | solution.py:82
  395.8 5.4 all_gather.20
  401.2 26.6 %all_gather.21 = f32[4,48,192]{1,2,0:T(8,128)S(1)} all-gather(f32[4,48,24]{1,2,0:T(8,128)S(1)} %all_gather.20), channel_id=1, replica_groups=mesh['sub'=8,'grp'=4] {'sub'}, dimensions={2}, use_global_device_ids=true | all-gather | bytes 165888 | tf_op jit(solution)/shard_map/all_gather | solution.py:102
  428.7 5.9 collective-permute-start.14
  437.8 43.5 %psum.45 = f32[48,48]{0,1:T(8,128)S(1)} all-reduce(f32[48,48]{0,1:T(8,128)S(1)} %convolution_bitcast_fusion.12), channel_id=1, replica_groups=mesh['sub'=8,'grp'=4] {'sub','grp'}, use_global_device_ids=true, to_apply=%region_5.0 | all-reduce | flops 2304 | bytes 18432 | tf_op jit(solution)/shard_map/psum | solution.py:111
  481.4 4.4 cholesky.111
  508.8 41.7 %psum.46 = f32[48,48]{1,0:T(8,128)S(1)} all-reduce(f32[48,48]{1,0:T(8,128)S(1)} %convolution_bitcast_fusion.11), channel_id=1, replica_groups=mesh['sub'=8,'grp'=4] {'sub','grp'}, use_global_device_ids=true, to_apply=%region_6.9 | all-reduce | flops 2304 | bytes 18432 | tf_op jit(solution)/shard_map/psum | solution.py:82
  561.3 5.4 all_gather.22
  566.7 26.5 %all_gather.23 = f32[4,48,192]{1,2,0:T(8,128)S(1)} all-gather(f32[4,48,24]{1,2,0:T(8,128)S(1)} %all_gather.22), channel_id=1, replica_groups=mesh['sub'=8,'grp'=4] {'sub'}, dimensions={2}, use_global_device_ids=true | all-gather | bytes 165888 | tf_op jit(solution)/shard_map/all_gather | solution.py:102
  594.2 5.9 collective-permute-start.22
  603.0 43.4 %psum.47 = f32[48,48]{0,1:T(8,128)S(1)} all-reduce(f32[48,48]{0,1:T(8,128)S(1)} %convolution_bitcast_fusion.10), channel_id=1, replica_groups=mesh['sub'=8,'grp'=4] {'sub','grp'}, use_global_device_ids=true, to_apply=%region_7.10 | all-reduce | flops 2304 | bytes 18432 | tf_op jit(solution)/shard_map/psum | solution.py:111
  646.4 4.4 cholesky.133
  (233 shorter events, 130.4 us)
Async XLA Ops:
  2.7 193.0 %collective-permute-start = (f32[1,48,256]{2,1,0:T(8,128)S(1)}, f32[1,48,256]{2,1,0:T(8,128)S(1)}, u32[]{:S(2)}, u32[]{:S(2)}) collective-permute-start(f32[1,48,256]{2,1,0:T(8,128)S(1)} %get-tuple-element.64), channel_id=1, source_target_pairs={{0,4},{4,8},{8,12},{12,16},{16,20},{20,24},{24,28},{1,5},{5,9},{9,... | collective-permute-start | bytes 147464 | tf_op jit(solution)/shard_map/ppermute | solution.py:15
  6.2 189.5 %collective-permute-start.1 = (f32[2,48,256]{2,1,0:T(8,128)S(1)}, f32[2,48,256]{2,1,0:T(8,128)S(1)}, u32[]{:S(2)}, u32[]{:S(2)}) collective-permute-start(f32[2,48,256]{2,1,0:T(8,128)S(1)} %slice_bitcast_fusion.5), channel_id=1, source_target_pairs={{3,0},{0,1},{1,2},{2,3},{7,4},{4,5},{5,6},{6,7},{11,8},{8,9},{9,10... | collective-permute-start | bytes 294920 | tf_op jit(solution)/shard_map/ppermute | solution.py:21
  199.6 7.1 %collective-permute-start.2 = (f32[1,48,256]{2,1,0:T(8,128)S(1)}, f32[1,48,256]{2,1,0:T(8,128)S(1)}, u32[]{:S(2)}, u32[]{:S(2)}) collective-permute-start(f32[1,48,256]{2,1,0:T(8,128)S(1)} %bitcast.587), channel_id=1, source_target_pairs={{4,0},{8,4},{12,8},{16,12},{20,16},{24,20},{28,24},{5,1},{9,5},{13... | collective-permute-start | bytes 147464 | tf_op jit(solution)/shard_map/ppermute | solution.py:15
  202.6 4.2 collective-permute-start.3
  206.9 6.2 collective-permute-start.4
  210.9 4.1 collective-permute-start.5
  249.1 6.9 %collective-permute-start.6 = (f32[1,48,256]{2,1,0:T(8,128)S(1)}, f32[1,48,256]{2,1,0:T(8,128)S(1)}, u32[]{:S(2)}, u32[]{:S(2)}) collective-permute-start(f32[1,48,256]{2,1,0:T(8,128)S(1)} %bitcast.588), channel_id=1, source_target_pairs={{4,0},{8,4},{12,8},{16,12},{20,16},{24,20},{28,24},{5,1},{9,5},{13... | collective-permute-start | bytes 147464 | tf_op jit(solution)/shard_map/ppermute | solution.py:15
  253.7 2.5 collective-permute-start.7
  311.2 11.4 %collective-permute-start.8 = (f32[1,48,256]{2,1,0:T(8,128)S(1)}, f32[1,48,256]{2,1,0:T(8,128)S(1)}, u32[]{:S(2)}, u32[]{:S(2)}) collective-permute-start(f32[1,48,256]{2,1,0:T(8,128)S(1)} %get-tuple-element.54), channel_id=1, source_target_pairs={{0,4},{4,8},{8,12},{12,16},{16,20},{20,24},{24,28},{1,5},{5,9},{9,... | collective-permute-start | bytes 147464 | tf_op jit(solution)/shard_map/ppermute | solution.py:15
  313.1 9.5 %collective-permute-start.9 = (f32[2,48,256]{2,1,0:T(8,128)S(1)}, f32[2,48,256]{2,1,0:T(8,128)S(1)}, u32[]{:S(2)}, u32[]{:S(2)}) collective-permute-start(f32[2,48,256]{2,1,0:T(8,128)S(1)} %slice_bitcast_fusion.3), channel_id=1, source_target_pairs={{3,0},{0,1},{1,2},{2,3},{7,4},{4,5},{5,6},{6,7},{11,8},{8,9},{9,10... | collective-permute-start | bytes 294920 | tf_op jit(solution)/shard_map/ppermute | solution.py:21
  326.6 6.9 %collective-permute-start.10 = (f32[1,48,256]{2,1,0:T(8,128)S(1)}, f32[1,48,256]{2,1,0:T(8,128)S(1)}, u32[]{:S(2)}, u32[]{:S(2)}) collective-permute-start(f32[1,48,256]{2,1,0:T(8,128)S(1)} %bitcast.589), channel_id=1, source_target_pairs={{4,0},{8,4},{12,8},{16,12},{20,16},{24,20},{28,24},{5,1},{9,5},{13... | collective-permute-start | bytes 147464 | tf_op jit(solution)/shard_map/ppermute | solution.py:15
  330.8 3.7 collective-permute-start.11
  381.6 6.3 collective-permute-start.12
  387.8 4.1 collective-permute-start.13
  428.7 7.7 %collective-permute-start.14 = (f32[1,48,256]{2,1,0:T(8,128)S(1)}, f32[1,48,256]{2,1,0:T(8,128)S(1)}, u32[]{:S(2)}, u32[]{:S(2)}) collective-permute-start(f32[1,48,256]{2,1,0:T(8,128)S(1)} %bitcast.590), channel_id=1, source_target_pairs={{4,0},{8,4},{12,8},{16,12},{20,16},{24,20},{28,24},{5,1},{9,5},{13... | collective-permute-start | bytes 147464 | tf_op jit(solution)/shard_map/ppermute | solution.py:15
  434.9 2.5 collective-permute-start.15
  491.6 6.0 collective-permute-start.16
  493.5 4.1 collective-permute-start.17
  501.5 6.9 %collective-permute-start.18 = (f32[1,48,256]{2,1,0:T(8,128)S(1)}, f32[1,48,256]{2,1,0:T(8,128)S(1)}, u32[]{:S(2)}, u32[]{:S(2)}) collective-permute-start(f32[1,48,256]{2,1,0:T(8,128)S(1)} %bitcast.591), channel_id=1, source_target_pairs={{4,0},{8,4},{12,8},{16,12},{20,16},{24,20},{28,24},{5,1},{9,5},{13... | collective-permute-start | bytes 147464 | tf_op jit(solution)/shard_map/ppermute | solution.py:15
  505.8 2.7 collective-permute-start.19
  551.3 6.0 collective-permute-start.20
  553.3 4.1 collective-permute-start.21
  594.2 7.6 %collective-permute-start.22 = (f32[1,48,256]{2,1,0:T(8,128)S(1)}, f32[1,48,256]{2,1,0:T(8,128)S(1)}, u32[]{:S(2)}, u32[]{:S(2)}) collective-permute-start(f32[1,48,256]{2,1,0:T(8,128)S(1)} %bitcast.592), channel_id=1, source_target_pairs={{4,0},{8,4},{12,8},{16,12},{20,16},{24,20},{28,24},{5,1},{9,5},{13... | collective-permute-start | bytes 147464 | tf_op jit(solution)/shard_map/ppermute | solution.py:15
  600.4 2.3 collective-permute-start.23
  (3 other events, 303.4 us)
where the time goes:
time: 662 us; the launch traced here: 658 us
  blocking collectives  308 us (47%)
  local copies, waits for them, and re-layouts  193 us (29%)
  other arithmetic  49.2 us (7%)
  starting transfers between devices  47 us (7%)
  matrix products  30.1 us (5%)
  waiting for transfers between devices  28.4 us (4%)
    gather x6, local copies, waits for them, and re-layouts, body(): permute = jax.vmap(lambda matrix, ordering: matrix[ordering][:, ordering])  177 us
    psum x3, blocking collectives, precondition(): lax.psum(pair_sum(filtered, resid, 'gksat,gksbt->ab'), ('sub', 'grp'))  126 us
    psum x2, blocking collectives, body(): lax.psum(pair_sum(direction, image_faces, 'gksat,gksbt->ab'), ('sub', 'gr...  86.9 us
    all_gather x3, blocking collectives, body(): lax.all_gather(cycle_terms, 'sub', axis=2, tiled=True)  79.3 us
    ppermute x12, starting transfers between devices, shifted(): lax.ppermute(value, axis, [(source, source + steps) for source in range(i...  41.7 us
    another operation x15, other arithmetic, gram_solve(): jnp.linalg.cholesky(matrix)  25.3 us
    another operation x10, other arithmetic, gram_solve(): jax.scipy.linalg.cho_solve((jnp.linalg.cholesky(matrix), True), right)  21.6 us
    ppermute x12, waiting for transfers between devices, shifted(): lax.ppermute(value, axis, [(source, source + steps) for source in range(i...  19.5 us
  transfers between devices with their start and end apart: 24, of which 15 were waited for; matrix products, arithmetic and copies ran while one was open for 31% of the time, Pallas kernels for 0%

commit v1 on v0

--- a/solution.py
+++ b/solution.py
@@ -108,7 +108,9 @@
             "krq,kqm->krm", corrections, coarse_basis, preferred_element_type=jnp.float32
         )
         image_faces = to_faces(response, live_mask)
-        curvature = lax.psum(pair_sum(direction, image_faces, "gksat,gksbt->ab"), ("sub", "grp"))
+        own = pair_sum(direction, image_faces, "gksat,gksbt->ab")
+        terms = lax.all_gather(own, ("sub", "grp"))
+        curvature = jnp.sum(terms, axis=0)
         image_faces, curvature = (image_faces, curvature)
         step_size = gram_solve(curvature, precond_gram)
         multipliers = multipliers + combine(step_size, direction)

time: 662 us -> 699 us (1.056)
  the two profiles are of different devices: /device:TPU:10 before, /device:TPU:0 now
where the time goes in v1:
time: 699 us; the launch traced here: 696 us
  blocking collectives  347 us (50%)
  local copies, waits for them, and re-layouts  194 us (28%)
  other arithmetic  49.5 us (7%)
  waiting for transfers between devices  37.1 us (5%)
  starting transfers between devices  36.3 us (5%)
  matrix products  30.1 us (4%)
    gather x6, local copies, waits for them, and re-layouts, body(): permute = jax.vmap(lambda matrix, ordering: matrix[ordering][:, ordering])  178 us
    all_gather x3, blocking collectives, body(): terms = lax.all_gather(own, ('sub', 'grp'))  121 us
    psum x3, blocking collectives, precondition(): lax.psum(pair_sum(filtered, resid, 'gksat,gksbt->ab'), ('sub', 'grp'))  117 us
    all_gather x3, blocking collectives, body(): lax.all_gather(cycle_terms, 'sub', axis=2, tiled=True)  93.4 us
    ppermute x12, starting transfers between devices, shifted(): lax.ppermute(value, axis, [(source, source + steps) for source in range(i...  30.9 us
    ppermute x12, waiting for transfers between devices, shifted(): lax.ppermute(value, axis, [(source, source + steps) for source in range(i...  26.1 us
    another operation x15, other arithmetic, gram_solve(): jnp.linalg.cholesky(matrix)  25.3 us
    another operation x10, other arithmetic, gram_solve(): jax.scipy.linalg.cho_solve((jnp.linalg.cholesky(matrix), True), right)  21.6 us
  transfers between devices with their start and end apart: 24, of which 13 were waited for; matrix products, arithmetic and copies ran while one was open for 30% of the time, Pallas kernels for 0%

profile of v1, /device:TPU:0, one launch (start us, length us, event | category | flops | bytes accessed | tf_op | source)
XLA Modules:
  0.0 695.8 jit_solution(12960999615292255584)
XLA Ops:
  2.7 4.8 collective-permute-start
  8.4 42.0 %gather_fusion = bf16[2048,1024]{1,0:T(8,128)(2,1)} fusion(bf16[2,1024,1024]{2,1,0:T(8,128)(2,1)} %bitcast.542, s32[2048]{0:T(1024)S(1)} %bitcast.537), kind=kCustom, calls=%fused_computation | custom fusion | bytes 8404992 | tf_op jit(solution)/shard_map/vmap()/gather | solution.py:57
  50.4 6.2 copy.165
  56.6 40.5 %gather_fusion.1 = bf16[2048,1024]{1,0:T(8,128)(2,1)} fusion(bf16[2,1024,1024]{1,2,0:T(8,128)(2,1)} %copy.165, s32[2048]{0:T(1024)S(1)} %bitcast.538), kind=kCustom, calls=%fused_computation.1 | custom fusion | bytes 8404992 | tf_op jit(solution)/shard_map/vmap()/gather | solution.py:57
  97.2 42.0 %gather_fusion.2 = bf16[2048,1024]{1,0:T(8,128)(2,1)} fusion(bf16[2,1024,1024]{2,1,0:T(8,128)(2,1)} %bitcast.543, s32[2048]{0:T(1024)S(1)} %bitcast.539), kind=kCustom, calls=%fused_computation.2 | custom fusion | bytes 8404992 | tf_op jit(solution)/shard_map/vmap()/gather | solution.py:57
  139.2 6.2 copy.176
  145.4 40.6 %gather_fusion.3 = bf16[2048,1024]{1,0:T(8,128)(2,1)} fusion(bf16[2,1024,1024]{1,2,0:T(8,128)(2,1)} %copy.176, s32[2048]{0:T(1024)S(1)} %bitcast.540), kind=kCustom, calls=%fused_computation.3 | custom fusion | bytes 8404992 | tf_op jit(solution)/shard_map/vmap()/gather | solution.py:57
  186.3 11.1 %gather_fusion.4 = bf16[2048,12]{1,0:T(8,128)(2,1)S(1)} fusion(bf16[2,12,1024]{1,2,0:T(8,128)(2,1)S(1)} %bitcast.561, s32[2048]{0:T(1024)S(1)} %bitcast.541), kind=kCustom, calls=%fused_computation.4 | custom fusion | bytes 114688 | tf_op jit(solution)/shard_map/vmap()/gather | solution.py:60
  217.8 5.2 all_gather.36
  223.0 31.3 %all_gather.37 = f32[4,48,192]{1,2,0:T(8,128)S(1)} all-gather(f32[4,48,24]{1,2,0:T(8,128)S(1)} %all_gather.36), channel_id=1, replica_groups=mesh['sub'=8,'grp'=4] {'sub'}, dimensions={2}, use_global_device_ids=true | all-gather | bytes 165888 | tf_op jit(solution)/shard_map/all_gather | solution.py:102
  262.0 40.3 %all-gather = f32[1536,48]{1,0:T(8,128)S(1)} all-gather(f32[48,48]{1,0:T(8,128)S(1)} %convolution_bitcast_fusion.15), channel_id=2, replica_groups=mesh['sub'=8,'grp'=4] {'sub','grp'}, dimensions={0}, use_global_device_ids=true | all-gather | bytes 304128 | tf_op jit(solution)/shard_map/all_gather | solution.py:112
  302.5 4.4 cholesky.89
  311.9 37.1 %psum.21 = f32[48,48]{0,1:T(8,128)S(1)} all-reduce(f32[48,48]{0,1:T(8,128)S(1)} %convolution_bitcast_fusion.14), channel_id=1, replica_groups=mesh['sub'=8,'grp'=4] {'sub','grp'}, use_global_device_ids=true, to_apply=%region_3.5 | all-reduce | flops 2304 | bytes 18432 | tf_op jit(solution)/shard_map/psum | solution.py:82
  374.2 41.8 %psum.22 = f32[48,48]{0,1:T(8,128)S(1)} all-reduce(f32[48,48]{0,1:T(8,128)S(1)} %convolution_bitcast_fusion.13), channel_id=1, replica_groups=mesh['sub'=8,'grp'=4] {'sub','grp'}, use_global_device_ids=true, to_apply=%region_4.0 | all-reduce | flops 2304 | bytes 18432 | tf_op jit(solution)/shard_map/psum | solution.py:82
  417.0 4.4 cholesky.122
  438.6 5.2 all_gather.40
  443.8 31.2 %all_gather.41 = f32[4,48,192]{1,2,0:T(8,128)S(1)} all-gather(f32[4,48,24]{1,2,0:T(8,128)S(1)} %all_gather.40), channel_id=1, replica_groups=mesh['sub'=8,'grp'=4] {'sub'}, dimensions={2}, use_global_device_ids=true | all-gather | bytes 165888 | tf_op jit(solution)/shard_map/all_gather | solution.py:102
  482.3 40.6 %all-gather.1 = f32[1536,48]{1,0:T(8,128)S(1)} all-gather(f32[48,48]{1,0:T(8,128)S(1)} %convolution_bitcast_fusion.12), channel_id=3, replica_groups=mesh['sub'=8,'grp'=4] {'sub','grp'}, dimensions={0}, use_global_device_ids=true | all-gather | bytes 304128 | tf_op jit(solution)/shard_map/all_gather | solution.py:112
  523.1 4.4 cholesky.111
  549.0 38.2 %psum.23 = f32[48,48]{1,0:T(8,128)S(1)} all-reduce(f32[48,48]{1,0:T(8,128)S(1)} %convolution_bitcast_fusion.11), channel_id=1, replica_groups=mesh['sub'=8,'grp'=4] {'sub','grp'}, use_global_device_ids=true, to_apply=%region_6.9 | all-reduce | flops 2304 | bytes 18432 | tf_op jit(solution)/shard_map/psum | solution.py:82
  600.3 5.2 all_gather.44
  605.5 31.0 %all_gather.45 = f32[4,48,192]{1,2,0:T(8,128)S(1)} all-gather(f32[4,48,24]{1,2,0:T(8,128)S(1)} %all_gather.44), channel_id=1, replica_groups=mesh['sub'=8,'grp'=4] {'sub'}, dimensions={2}, use_global_device_ids=true | all-gather | bytes 165888 | tf_op jit(solution)/shard_map/all_gather | solution.py:102
  643.8 39.9 %all-gather.2 = f32[1536,48]{1,0:T(8,128)S(1)} all-gather(f32[48,48]{1,0:T(8,128)S(1)} %convolution_bitcast_fusion.10), channel_id=4, replica_groups=mesh['sub'=8,'grp'=4] {'sub','grp'}, dimensions={0}, use_global_device_ids=true | all-gather | bytes 304128 | tf_op jit(solution)/shard_map/all_gather | solution.py:112
  683.9 4.4 cholesky.133
  (237 shorter events, 135.5 us)
Async XLA Ops:
  2.7 194.8 %collective-permute-start = (f32[1,48,256]{2,1,0:T(8,128)S(1)}, f32[1,48,256]{2,1,0:T(8,128)S(1)}, u32[]{:S(2)}, u32[]{:S(2)}) collective-permute-start(f32[1,48,256]{2,1,0:T(8,128)S(1)} %get-tuple-element.62), channel_id=1, source_target_pairs={{0,4},{4,8},{8,12},{12,16},{16,20},{20,24},{24,28},{1,5},{5,9},{9,... | collective-permute-start | bytes 147464 | tf_op jit(solution)/shard_map/ppermute | solution.py:15
  7.6 189.9 %collective-permute-start.1 = (f32[2,48,256]{2,1,0:T(8,128)S(1)}, f32[2,48,256]{2,1,0:T(8,128)S(1)}, u32[]{:S(2)}, u32[]{:S(2)}) collective-permute-start(f32[2,48,256]{2,1,0:T(8,128)S(1)} %slice_bitcast_fusion.5), channel_id=1, source_target_pairs={{3,0},{0,1},{1,2},{2,3},{7,4},{4,5},{5,6},{6,7},{11,8},{8,9},{9,10... | collective-permute-start | bytes 294920 | tf_op jit(solution)/shard_map/ppermute | solution.py:21
  201.4 6.4 collective-permute-start.2
  203.3 4.6 collective-permute-start.3
  207.9 5.9 collective-permute-start.4
  212.0 4.1 collective-permute-start.5
  255.3 6.0 collective-permute-start.6
  256.9 4.4 collective-permute-start.7
  350.2 13.7 %collective-permute-start.8 = (f32[1,48,256]{2,1,0:T(8,128)S(1)}, f32[1,48,256]{2,1,0:T(8,128)S(1)}, u32[]{:S(2)}, u32[]{:S(2)}) collective-permute-start(f32[1,48,256]{2,1,0:T(8,128)S(1)} %get-tuple-element.52), channel_id=1, source_target_pairs={{0,4},{4,8},{8,12},{12,16},{16,20},{20,24},{24,28},{1,5},{5,9},{9,... | collective-permute-start | bytes 147464 | tf_op jit(solution)/shard_map/ppermute | solution.py:15
  354.4 9.5 %collective-permute-start.9 = (f32[2,48,256]{2,1,0:T(8,128)S(1)}, f32[2,48,256]{2,1,0:T(8,128)S(1)}, u32[]{:S(2)}, u32[]{:S(2)}) collective-permute-start(f32[2,48,256]{2,1,0:T(8,128)S(1)} %slice_bitcast_fusion.3), channel_id=1, source_target_pairs={{3,0},{0,1},{1,2},{2,3},{7,4},{4,5},{5,6},{6,7},{11,8},{8,9},{9,10... | collective-permute-start | bytes 294920 | tf_op jit(solution)/shard_map/ppermute | solution.py:21
  367.8 6.0 collective-permute-start.10
  369.4 4.5 collective-permute-start.11
  422.1 8.5 %collective-permute-start.12 = (f32[1,48,256]{2,1,0:T(8,128)S(1)}, f32[1,48,256]{2,1,0:T(8,128)S(1)}, u32[]{:S(2)}, u32[]{:S(2)}) collective-permute-start(f32[1,48,256]{2,1,0:T(8,128)S(1)} %get-tuple-element.46), channel_id=1, source_target_pairs={{0,4},{4,8},{8,12},{12,16},{16,20},{20,24},{24,28},{1,5},{5,9},{9,... | collective-permute-start | bytes 147464 | tf_op jit(solution)/shard_map/ppermute | solution.py:15
  430.6 4.1 collective-permute-start.13
  476.0 6.0 collective-permute-start.14
  477.8 4.2 collective-permute-start.15
  533.3 3.1 collective-permute-start.16
  534.6 4.1 collective-permute-start.17
  542.7 6.0 collective-permute-start.18
  544.2 4.4 collective-permute-start.19
  588.0 5.9 collective-permute-start.20
  592.2 4.1 collective-permute-start.21
  637.5 6.0 collective-permute-start.22
  639.0 4.4 collective-permute-start.23
  (3 other events, 309.1 us)
